TPU v7x, 256 devices: a whole 4x4x8 slice. The times are simulated.
256 devices in a mesh: rows: 64 (over z, y, core), nbr: 4 (over x).
Axes of the slice: x: 4, y: 4, z: 8, core: 2. Of those that a mesh axis runs over, the one named last changes fastest.
Arguments:
- expression: bfloat16 [1024, 128, 128], P('rows'), may hold values from -80 to 80
- nbr_owner: int32 [4, 1024, 4], replicated, may hold values from 0 to 63, all different within a row; in each aligned block of 16 rows (0 to 15, 16 to 31, ..., all dimensions but the last counted through in order) at most 2 rows name the same one
- nbr_slot: int32 [4, 1024, 4], replicated, may hold values from 0 to 15
Outputs:
- intersection_tiles: float32 [1024, 16, 128, 128], P('rows', 'nbr')
Inputs may be any that keep to these rules, and one draw needn't show every extreme that they name: `nbr_owner`: each row (n, b) names 4 different owners. Within the 16 rows b of one device's bands for one n, no owner is named more than 2 times, and in some such groups an owner is named exactly 2 times.
All inputs are finite; a program needn't handle non-finite values.
Results may differ from a plain program's by a relative error of at most 0.01.
Values may be sent and summed in bfloat16 or wider, within the bound.
A program may use at most 128 MiB of HBM per device.

v0:
```python
import jax
import jax.numpy as jnp
from jax import lax
from jax.sharding import PartitionSpec as P


def standardize(blocks):
    values = blocks.astype(jnp.float32)
    centred = values - jnp.mean(values, axis=-1, keepdims=True)
    inverse_norm = lax.rsqrt(jnp.sum(centred * centred, axis=-1, keepdims=True) + 1e-06)
    return (centred * inverse_norm).astype(jnp.bfloat16)


def power_twelve(correlation):
    base = 0.5 + 0.5 * correlation
    second = base * base
    fourth = second * second
    eighth = fourth * fourth
    return eighth * fourth


def adjacency(left_rows, right_rows, same_block):
    correlation = jnp.einsum(
        "uvs,cjs->uvcj", left_rows, right_rows, preferred_element_type=jnp.float32
    )
    soft_value = power_twelve(correlation)
    diagonal = jnp.eye(left_rows.shape[1], dtype=bool)
    zeroed = same_block[:, None, :, None] & diagonal[None, :, None, :]
    return jnp.where(zeroed, 0.0, soft_value).astype(jnp.bfloat16)


def first_weights(band_lists, band_ids):
    length = band_lists.shape[1]
    position = jnp.arange(length, dtype=jnp.int32)
    earlier = position[None, :] < position[:, None]
    repeated = jnp.any((band_lists[:, :, None] == band_lists[:, None, :]) & earlier[None], axis=2)
    return ((band_lists != band_ids[:, None]) & jnp.logical_not(repeated)).astype(jnp.float32)


def send_plan(owners, slots, row_index, rows_count, capacity):
    owner_hit = (owners.reshape(rows_count, -1) == row_index).astype(jnp.int32)
    place_rank = jnp.cumsum(owner_hit, axis=1) - 1
    chosen = (owner_hit[:, None, :] == 1) & (
        place_rank[:, None, :] == jnp.arange(capacity, dtype=jnp.int32)[None, :, None]
    )
    slot_index = jnp.sum(jnp.where(chosen, slots.reshape(rows_count, 1, -1), 0), axis=2)
    present = jnp.any(chosen, axis=2)
    return (slot_index, present)


def receive_rank(owners):
    length = owners.shape[0]
    position = jnp.arange(length, dtype=jnp.int32)
    earlier = position[None, :] < position[:, None]
    return jnp.sum((owners[:, None] == owners[None, :]) & earlier, axis=1)


def per_device(expression, nbr_owner, nbr_slot):
    rows_count = lax.axis_size("rows")
    groups = lax.axis_size("nbr")
    row_index = lax.axis_index("rows")
    group_index = lax.axis_index("nbr")
    band_count, block_rows, samples = expression.shape
    per_group = nbr_owner.shape[2]
    list_len = groups * per_group
    capacity = max(2, min(band_count, 2 * band_count * per_group // rows_count))
    zscores = standardize(expression)
    block_ids = nbr_owner * band_count + nbr_slot
    my_owner = lax.dynamic_slice_in_dim(nbr_owner, row_index * band_count, band_count, 1)
    my_ids = lax.dynamic_slice_in_dim(block_ids, row_index * band_count, band_count, 1)
    band_lists = jnp.transpose(my_ids, (1, 0, 2)).reshape(band_count, list_len)
    band_ids = row_index * band_count + jnp.arange(band_count, dtype=jnp.int32)
    weights = first_weights(band_lists, band_ids)
    part_owner = lax.dynamic_index_in_dim(nbr_owner, group_index, 0, keepdims=False)
    part_slot = lax.dynamic_index_in_dim(nbr_slot, group_index, 0, keepdims=False)
    part_index, part_present = send_plan(part_owner, part_slot, row_index, rows_count, capacity)
    my_part_owner = lax.dynamic_slice_in_dim(
        part_owner, row_index * band_count, band_count, 0
    ).reshape(-1)
    part_spot = my_part_owner * capacity + receive_rank(my_part_owner)
    empty_rows = jnp.zeros((), jnp.bfloat16)
    outgoing = []
    for slice_number in range(groups):
        slot_index, present = send_plan(
            nbr_owner[slice_number], nbr_slot[slice_number], row_index, rows_count, capacity
        )
        outgoing.append(jnp.where(present[:, :, None, None], zscores[slot_index], empty_rows))
    incoming = lax.all_to_all(
        jnp.concatenate(outgoing, axis=1), "rows", split_axis=0, concat_axis=0, tiled=True
    )
    flat_rows = incoming.reshape(rows_count * groups * capacity, block_rows, samples)
    pieces = []
    for slice_number in range(groups):
        owners_mine = my_owner[slice_number].reshape(-1)
        spot_index = (
            owners_mine * (groups * capacity) + slice_number * capacity + receive_rank(owners_mine)
        )
        pieces.append(flat_rows[spot_index].reshape(band_count, per_group, block_rows, samples))
    neighbours = jnp.concatenate(pieces, axis=1)
    stacked = jnp.concatenate([zscores[:, None], neighbours], axis=1)
    correlation = jnp.einsum("bis,bujs->biuj", zscores, stacked, preferred_element_type=jnp.float32)
    same_row = jnp.concatenate(
        [jnp.ones((band_count, 1), bool), band_lists == band_ids[:, None]], axis=1
    )
    diagonal = jnp.eye(block_rows, dtype=bool)
    zeroed = same_row[:, None, :, None] & diagonal[None, :, None, :]
    rows_all = jnp.where(zeroed, 0.0, power_twelve(correlation)).astype(jnp.bfloat16)
    full_weights = jnp.concatenate(
        [jnp.ones((band_count, 1), jnp.float32), weights], axis=1
    ).astype(jnp.bfloat16)
    degrees = jnp.einsum("biuj,bu->bi", rows_all, full_weights, preferred_element_type=jnp.float32)
    degree_send = jnp.where(part_present[:, :, None], degrees[part_index], 0.0)
    received = (
        lax.all_to_all(
            degree_send.astype(jnp.bfloat16), "rows", split_axis=0, concat_axis=0, tiled=True
        )
        .astype(degree_send.dtype)
        .reshape(rows_count * capacity, block_rows)
    )
    near_degree = received[part_spot].reshape(band_count, per_group, block_rows)
    first_k = group_index * per_group

    def shared_terms(inputs):
        band_row, near_rows, list_row, weight_row = inputs
        own_rows = lax.dynamic_slice_in_dim(near_rows, first_k, per_group, 0)
        own_ids = lax.dynamic_slice_in_dim(list_row, first_k, per_group, 0)
        own_weight = lax.dynamic_slice_in_dim(weight_row, first_k, per_group, 0).astype(
            jnp.bfloat16
        )
        pair_tiles = adjacency(own_rows, near_rows, own_ids[:, None] == list_row[None, :])
        lead_tiles = (
            lax.dynamic_slice_in_dim(band_row, 1 + first_k, per_group, 1)
            * own_weight[None, :, None]
        )
        partial_terms = jnp.dot(
            lead_tiles.reshape(block_rows, per_group * block_rows),
            pair_tiles.reshape(per_group * block_rows, list_len * block_rows),
            preferred_element_type=jnp.float32,
        )
        self_term = jnp.dot(
            band_row[:, 0, :],
            band_row[:, 1:, :].reshape(block_rows, list_len * block_rows),
            preferred_element_type=jnp.float32,
        )
        partial_terms = partial_terms + jnp.where(group_index == 0, 1.0, 0.0) * self_term
        return partial_terms.reshape(block_rows, list_len, block_rows)

    partial_value = lax.map(shared_terms, (rows_all, neighbours, band_lists, weights))
    shared = lax.psum_scatter(
        partial_value.astype(jnp.bfloat16), "nbr", scatter_dimension=2, tiled=True
    ).astype(jnp.float32)
    link_tiles = lax.dynamic_slice_in_dim(rows_all, 1 + first_k, per_group, 2).astype(jnp.float32)
    lower_degree = jnp.minimum(degrees[:, :, None, None], near_degree[:, None, :, :])
    intersection_tiles = (shared + link_tiles) / (lower_degree + 1.0 - link_tiles)
    return jnp.transpose(intersection_tiles, (0, 2, 1, 3))


def solution(mesh):
    placed = (P("rows", None, None), P(), P())
    return jax.shard_map(
        per_device,
        mesh=mesh,
        in_specs=placed,
        out_specs=P("rows", "nbr", None, None),
        check_vma=False,
    )
```

profile of v0, /device:TPU:1, one launch (start us, length us, event | category | flops | bytes accessed | tf_op | source)
XLA Modules:
  0.0 807.2 jit_solution(9347710504580656433)
XLA Ops:
  16.8 3.1 gather_fusion.3
  19.9 3.0 gather_fusion.2
  23.3 3.1 gather_fusion.1
  27.5 3.1 gather_fusion
  38.8 7.1 pad_maximum_fusion
  45.9 13.3 %all-to-all-start = ((bf16[64,8,128,128]{3,2,1,0:T(8,128)(2,1)}), bf16[64,8,128,128]{3,2,1,0:T(8,128)(2,1)}, u32[]{:S(2)}, u32[]{:S(2)}) async-start(bf16[64,8,128,128]{3,2,1,0:T(8,128)(2,1)} %pad_maximum_fusion), calls=%async_computation | async-start | bytes 33554432 | tf_op jit(solution)/shard_map/all_to_all | solution.py:88
  64.1 359.3 %all-to-all-done = bf16[64,8,128,128]{3,2,1,0:T(8,128)(2,1)} async-done(((bf16[64,8,128,128]{3,2,1,0:T(8,128)(2,1)}), bf16[64,8,128,128]{3,2,1,0:T(8,128)(2,1)}, u32[]{:S(2)}, u32[]{:S(2)}) %all-to-all-start) | async-done | bytes 16777248 | tf_op jit(solution)/shard_map/all_to_all | solution.py:88
  423.4 7.9 gather_fusion.5
  431.3 7.9 gather_fusion.6
  439.2 6.7 gather_fusion.7
  445.9 7.9 gather_fusion.4
  453.8 3.8 constant_dynamic-update-slice_fusion.4
  459.6 4.4 pad_maximum_fusion.1
  466.7 9.1 %convert_reduce_fusion = (bf16[16,128,17]{1,2,0:T(8,128)(2,1)S(1)}, bf16[16,128,17,128]{1,3,2,0:T(8,128)(2,1)}) fusion(bf16[16,17,128,128]{3,2,1,0:T(8,128)(2,1)S(1)} %constant_dynamic-update-slice_fusion.1, bf16[16,128,128]{2,1,0:T(8,128)(2,1)S(1)} %get-tuple-element.261, pred[128,128]{0,1:T(8,128)(4,1)S(1)} %iota_compare_fusion.6, ...), kind=kOutput, calls=%fused_computation.36 | convolution fusion | flops 1189836800 | bytes 18436368 | tf_op jit(solution)/shard_map/bis,bujs->biuj/dot_general | solution.py:101
  475.8 143.9 %while.13 = (s32[]{:T(128)}, bf16[16,128,16,128]{1,3,2,0:T(8,128)(2,1)}, bf16[16,128,17,128]{1,3,2,0:T(8,128)(2,1)}, s32[]{:T(128)}, bf16[16,16]{1,0:T(8,128)(2,...) while((s32[]{:T(128)}, ...), condition=%wide.region_20.21_spmd, body=%wide.region_19.20_spmd.sunk | while | flops 614285376 | bytes 19073076 | solution.py:148
  484.9 2.7 fusion.68
  493.9 2.7 fusion.68
  556.8 2.7 fusion.68
  565.8 2.7 fusion.68
  623.6 15.0 %all-to-all-start.1 = ((bf16[64,2,128]{2,1,0:T(2,128)(2,1)}), bf16[64,2,128]{2,1,0:T(2,128)(2,1)S(1)}, u32[]{:S(2)}, u32[]{:S(2)}) async-start(bf16[64,2,128]{2,1,0:T(2,128)(2,1)} %select_convert_fusion), calls=%async_computation.1 | async-start | bytes 65536 | tf_op jit(solution)/shard_map/all_to_all | solution.py:114
  638.6 9.3 %all-to-all-done.1 = bf16[64,2,128]{2,1,0:T(2,128)(2,1)S(1)} async-done(((bf16[64,2,128]{2,1,0:T(2,128)(2,1)}), bf16[64,2,128]{2,1,0:T(2,128)(2,1)S(1)}, u32[]{:S(2)}, u32[]{:S(2)}) %all-to-all-start.1) | async-done | bytes 32800 | tf_op jit(solution)/shard_map/all_to_all | solution.py:114
  648.5 142.3 %all-reduce.5.cloned.1.call-done = bf16[16,128,16,128]{1,3,2,0:T(8,128)(2,1)} async-done(((bf16[16,128,16,128]{1,3,2,0:T(8,128)(2,1)}), bf16[16,128,16,128]{1,3,2,0:T(8,128)(2,1)}) %all-reduce.5.cloned.1.call-update) | async-done | bytes 8388624
  790.8 4.2 fusion.15
  795.0 5.3 copy.166
  (406 shorter events, 165.0 us)
Async XLA Ops:
  6.5 4.5 copy-start.7
  7.6 5.1 copy-start.6
  30.7 3.4 copy-start.3
  34.1 2.2 copy-start.4
  36.3 2.2 copy-start.5
  45.9 377.5 %all-to-all-start = ((bf16[64,8,128,128]{3,2,1,0:T(8,128)(2,1)}), bf16[64,8,128,128]{3,2,1,0:T(8,128)(2,1)}, u32[]{:S(2)}, u32[]{:S(2)}) async-start(bf16[64,8,128,128]{3,2,1,0:T(8,128)(2,1)} %pad_maximum_fusion), calls=%async_computation | async-start | bytes 33554432 | tf_op jit(solution)/shard_map/all_to_all | solution.py:88
  59.3 731.5 %all-reduce.5.cloned.1.call-start = ((), (), s32[]{:S(2)}) async-start(), calls=%async_computation.2 | async-start | bytes 16777216
  453.8 3.8 copy-start.1
  453.8 5.7 copy-start
  453.8 5.7 copy-start.2
  459.6 6.4 copy-start.8
  619.6 0.9 copy-start.9
  623.6 24.3 %all-to-all-start.1 = ((bf16[64,2,128]{2,1,0:T(2,128)(2,1)}), bf16[64,2,128]{2,1,0:T(2,128)(2,1)S(1)}, u32[]{:S(2)}, u32[]{:S(2)}) async-start(bf16[64,2,128]{2,1,0:T(2,128)(2,1)} %select_convert_fusion), calls=%async_computation.1 | async-start | bytes 65536 | tf_op jit(solution)/shard_map/all_to_all | solution.py:114
Sparse Core Ops, SparseCore 0:
  619.8 170.9 all-reduce.4
where the time goes:
time: 809 us; the launch traced here: 807 us
  waiting for transfers between devices  511 us (63%)
  local copies, waits for them, and re-layouts  141 us (17%)
  matrix products  65 us (8%)
  other arithmetic  46.1 us (6%)
  starting transfers between devices  28.6 us (4%)
  between operations  14.6 us (2%)
    all_to_all x1, waiting for transfers between devices, per_device(): lax.all_to_all(jnp.concatenate(outgoing, axis=1), 'rows', split_axis=0, c...  359 us
    unnamed x2, waiting for transfers between devices  142 us
    dot_general x16, matrix products, adjacency(): jnp.einsum('uvs,cjs->uvcj', left_rows, right_rows, preferred_element_type...  43.3 us
    gather x4, local copies, waits for them, and re-layouts, per_device(): flat_rows[spot_index].reshape(band_count, per_group, block_rows, samples)  30.4 us
    dynamic_slice x32, local copies, waits for them, and re-layouts, per_device(): lax.map(shared_terms, (rows_all, neighbours, band_lists, weights))  22.5 us
    convert_element_type x16, local copies, waits for them, and re-layouts, adjacency(): return jnp.where(zeroed, 0.0, soft_value).astype(jnp.bfloat16)  21.7 us
    dynamic_update_slice x32, local copies, waits for them, and re-layouts, per_device(): lax.map(shared_terms, (rows_all, neighbours, band_lists, weights))  17.8 us
  transfers between devices with their start and end apart: 3, of which 3 were waited for; matrix products, arithmetic and copies ran while one was open for 1% of the time, Pallas kernels for 0%

commit v1 on v0

v1 whole, which is shorter than its diff:
```python
import heapq

import jax
import jax.numpy as jnp
from jax import lax
from jax.experimental import pallas as pl
from jax.experimental.pallas import tpu as pltpu
from jax.sharding import PartitionSpec as P

MESH = pl.DeviceIdType.MESH
BLOCK = 128
BANDS = 16
LIST = 16
OWN = 4
ZS, YS, XS = 8, 4, 4
CHIPS = ZS * YS
SHARD = BANDS * BLOCK
HALF = CHIPS * SHARD
PIECE = {"A": 704, "B": 672}
START = {"A": 0, "B": 704, "C": 704 + 672}
WIDTH = LIST * BLOCK + BLOCK
OWN_WIDTH = OWN * BLOCK
NT = (((1,), (1,)), ((), ()))


def piece_rows(kind, part):
    rows = PIECE["A" if kind == "A" else "B"]
    return rows if part == "f" else rows // 2


def next_sends(kind, part, dy, dz):
    sends = []
    if kind == "C":
        return sends
    first, second = part in "fa", part in "fb"
    along_z, along_y = [], []
    if 0 <= dz < 3:
        along_z.append(("z+", kind, part, dy, dz + 1))
    if dz == 3 and first:
        along_z.append(("z+", kind, "a", dy, 4))
    if -3 < dz <= 0:
        along_z.append(("z-", kind, part, dy, dz - 1))
    if dz == -3 and second:
        along_z.append(("z-", kind, "b", dy, -4))
    if dy == 0:
        along_y += [("y+", kind, part, 1, dz), ("y-", kind, part, -1, dz)]
    if dy == 1 and first:
        along_y.append(("y+", kind, "a", 2, dz))
    if dy == -1 and second:
        along_y.append(("y-", kind, "b", -2, dz))
    if kind == "A":
        sends += along_y if dz == 0 else []
        sends += along_z
    else:
        sends += along_z if dy == 0 else []
        sends += along_y
        if dy or dz:
            sends.append(("x+" if dz % 2 == 0 else "x-", "C", part, dy, dz))
    return sends


def gather_plan():
    free, heap, order, count, clock = {}, [], [], 0, 0.0
    for kind in ("B", "A"):
        heapq.heappush(heap, (0.0, count, (None, kind, "f", 0, 0)))
        count += 1
    while heap:
        time, _, event = heapq.heappop(heap)
        order.append(event)
        clock = max(clock, time) + 0.1
        for send in next_sends(*event[1:]):
            began = max(free.get(send[0], 0.0), clock)
            free[send[0]] = began + 2 * piece_rows(send[1], send[2]) * 256 / 115e3
            heapq.heappush(heap, (free[send[0]] + 2.5, count, send))
            count += 1
    return order


PLAN = gather_plan()
ARRIVALS = {event: number for number, event in enumerate(PLAN)}


def standardize_into(x_ref, z_all, mine):
    def one(i, carry):
        values = x_ref[i].astype(jnp.float32)
        centred = values - jnp.mean(values, axis=-1, keepdims=True)
        inverse = lax.rsqrt(jnp.sum(centred * centred, axis=-1, keepdims=True) + 1e-06)
        z_all[pl.ds(pl.multiple_of(mine + i * BLOCK, BLOCK), BLOCK), :] = (centred * inverse).astype(
            jnp.bfloat16
        )
        return carry

    lax.fori_loop(0, BANDS, one, 0)


def off_diagonal(dtype):
    i = lax.broadcasted_iota(jnp.int32, (BLOCK, BLOCK), 0)
    j = lax.broadcasted_iota(jnp.int32, (BLOCK, BLOCK), 1)
    return jnp.where(i == j, 0.0, 1.0).astype(dtype)


def block_of(z_all, block):
    return z_all[pl.ds(block * BLOCK, BLOCK), :]


def lead_band(b, my_block, block_ref, weight_ref, same_ref, z_all, lead, own_tiles):
    band = block_of(z_all, my_block + b)
    left = band * jnp.bfloat16(0.5)
    at = pl.ds(pl.multiple_of(b * BLOCK, BLOCK), BLOCK)
    apart = off_diagonal(jnp.float32)
    total = jnp.zeros((BLOCK, BLOCK), jnp.float32)
    for begin, end in ((0, 5), (5, 9), (9, 13), (13, 17)):
        right = [
            band if u == 0 else block_of(z_all, block_ref[b, u - 1]) for u in range(begin, end)
        ]
        base = 0.5 + lax.dot_general(
            left, jnp.concatenate(right, axis=0), NT, preferred_element_type=jnp.float32
        )
        second = base * base
        fourth = second * second
        soft = fourth * fourth * fourth
        for u in range(begin, end):
            tile = soft[:, (u - begin) * BLOCK : (u - begin + 1) * BLOCK]
            if u == 0:
                tile = tile * apart
            else:
                if u <= OWN:
                    tile = tile * (1.0 - same_ref[b, u - 1] * (1.0 - apart))
                    own_tiles[at, (u - 1) * BLOCK : u * BLOCK] = tile.astype(jnp.bfloat16)
                tile = tile * weight_ref[b, u - 1]
            lead[at, u * BLOCK : (u + 1) * BLOCK] = tile.astype(jnp.bfloat16)
            total = total + tile
    return jnp.sum(jnp.transpose(total), axis=0, keepdims=True)


def shared_band(b, block_ref, z_all, lead, own_tiles, pair):
    at = pl.ds(pl.multiple_of(b * BLOCK, BLOCK), BLOCK)
    own = [block_of(z_all, block_ref[b, c]) for c in range(OWN)]
    right = jnp.concatenate(own, axis=0) * jnp.bfloat16(0.5)
    apart = off_diagonal(jnp.bfloat16)
    links = own_tiles[at, :]
    pair[0:BLOCK, :] = links
    for u in range(0, LIST, 2):
        left = jnp.concatenate([block_of(z_all, block_ref[b, u + i]) for i in (0, 1)], axis=0)
        base = 0.5 + lax.dot_general(left, right, NT, preferred_element_type=jnp.float32)
        second = base * base
        fourth = (second * second).astype(jnp.bfloat16)
        soft = fourth * fourth * fourth
        top = (u + 1) * BLOCK
        pair[top : top + 2 * BLOCK, :] = soft
        if u < OWN:
            for i in (0, 1):
                c = u + i
                pair[top + i * BLOCK : top + (i + 1) * BLOCK, c * BLOCK : (c + 1) * BLOCK] = (
                    soft[i * BLOCK : (i + 1) * BLOCK, c * BLOCK : (c + 1) * BLOCK] * apart
                )
    shared = jnp.dot(lead[at, :], pair[...], preferred_element_type=jnp.float32)
    return shared + links.astype(jnp.float32)


def kernel(
    x_ref, block_ref, weight_ref, same_ref,
    sum_out, link_out, degree_out,
    z_all, lead, own_tiles, sums, degrees, pair,
    piece_recv, piece_send, core_recv, core_send, degree_recv, degree_send, out_sem,
):
    row = lax.axis_index("rows")
    plane = lax.axis_index("nbr")
    core, chip = row % 2, row // 2
    y, z = chip % YS, chip // YS
    odd = plane % 2

    def device(to_z, to_y):
        return (((to_z + ZS) % ZS * YS + (to_y + YS) % YS) * 2 + core, plane)

    links = {
        "z+": device(z + 1, y), "z-": device(z - 1, y),
        "y+": device(z, y + 1), "y-": device(z, y - 1),
        "x+": (row, (plane + 1) % XS), "x-": (row, (plane + XS - 1) % XS),
    }
    other = (chip * 2 + 1 - core, plane)
    barrier = pltpu.get_barrier_semaphore()
    for neighbour in list(links.values()) + [other]:
        pl.semaphore_signal(barrier, inc=1, device_id=neighbour, device_id_type=MESH)
    mine = core * HALF + chip * SHARD
    standardize_into(x_ref, z_all, mine)
    pl.semaphore_wait(barrier, 7)

    starts = {
        "A": START["A"],
        "B": START["B"] + odd * (START["C"] - START["B"]),
        "C": START["C"] - odd * (START["C"] - START["B"]),
    }

    def rows_at(kind, part, dy, dz):
        owner = (z - dz + ZS) % ZS * YS + (y - dy + YS) % YS
        rows = piece_rows(kind, part)
        first = core * HALF + owner * SHARD + starts[kind] + (rows if part == "b" else 0)
        return z_all.at[pl.ds(pl.multiple_of(first, 16), rows)]

    def copy(ref, send, recv, to):
        return pltpu.make_async_remote_copy(
            src_ref=ref, dst_ref=ref, send_sem=send, recv_sem=recv, device_id=to, device_id_type=MESH
        )

    shard = z_all.at[pl.ds(pl.multiple_of(mine, SHARD), SHARD)]
    sent_rows = 0
    for event in PLAN:
        link, kind, part, dy, dz = event
        ref = rows_at(kind, part, dy, dz)
        if link is not None:
            copy(ref, piece_send, piece_recv.at[ARRIVALS[event]], links[link]).wait_recv()
        for send in next_sends(kind, part, dy, dz):
            src = rows_at(kind, send[2], dy, dz)
            sent_rows += piece_rows(kind, send[2])
            copy(src, piece_send, piece_recv.at[ARRIVALS[send]], links[send[0]]).start()
        if link is not None:
            copy(ref, core_send, core_recv, other).start()
        elif kind == "A":
            copy(shard, core_send, core_recv, other).start()

    def drain(sem, first, rows):
        ref = z_all.at[pl.ds(first, rows)]
        pltpu.make_async_copy(ref, ref, sem).wait()

    drain(core_recv, pl.multiple_of((1 - core) * HALF, HALF), HALF)

    column = core * (CHIPS * BANDS) + y * (ZS * BANDS)
    my_degrees = column + z * BANDS

    def lead_step(b, carry):
        degrees[pl.ds(my_degrees + b, 1), :] = lead_band(
            b, mine // BLOCK, block_ref, weight_ref, same_ref, z_all, lead, own_tiles
        )
        return carry

    lax.fori_loop(0, BANDS, lead_step, 0)
    link_copy = pltpu.make_async_copy(own_tiles, link_out, out_sem.at[1])
    link_copy.start()

    def along_z(dz, part):
        rows = BANDS if part == "f" else BANDS // 2
        first = column + (z - dz + ZS) % ZS * BANDS + (rows if part == "b" else 0)
        return degrees.at[pl.ds(pl.multiple_of(first, 8), rows)]

    def along_y(dy, part):
        rows = ZS * BANDS if part == "f" else ZS * BANDS // 2
        first = (
            core * (CHIPS * BANDS) + (y - dy + YS) % YS * (ZS * BANDS) + (rows if part == "b" else 0)
        )
        return degrees.at[pl.ds(pl.multiple_of(first, 8), rows)]

    def hop(number, ref, link):
        return copy(ref, degree_send.at[number], degree_recv.at[number], links[link])

    def passes(number):
        if number < 3:
            d = number
            return [
                (hop(2 * d, along_z(d, "f"), "z+"), hop(2 * d, along_z(d + 1, "f"), "z+")),
                (hop(2 * d + 1, along_z(-d, "f"), "z-"), hop(2 * d + 1, along_z(-d - 1, "f"), "z-")),
            ]
        if number == 3:
            return [
                (hop(6, along_z(3, "a"), "z+"), hop(6, along_z(4, "a"), "z+")),
                (hop(7, along_z(-3, "b"), "z-"), hop(7, along_z(-4, "b"), "z-")),
            ]
        if number == 4:
            return [
                (hop(8, along_y(0, "f"), "y+"), hop(8, along_y(1, "f"), "y+")),
                (hop(9, along_y(0, "f"), "y-"), hop(9, along_y(-1, "f"), "y-")),
            ]
        if number == 5:
            return [
                (hop(10, along_y(1, "a"), "y+"), hop(10, along_y(2, "a"), "y+")),
                (hop(11, along_y(-1, "b"), "y-"), hop(11, along_y(-2, "b"), "y-")),
            ]
        part = degrees.at[pl.ds(pl.multiple_of(core * (CHIPS * BANDS), CHIPS * BANDS), CHIPS * BANDS)]
        back = degrees.at[
            pl.ds(pl.multiple_of((1 - core) * (CHIPS * BANDS), CHIPS * BANDS), CHIPS * BANDS)
        ]
        return [
            (copy(part, degree_send.at[12], degree_recv.at[12], other),
             copy(back, degree_send.at[12], degree_recv.at[12], other)),
        ]

    rounds = 7

    def exchange(number):
        if number > 0:
            for sent, came in passes(number - 1):
                sent.wait_send()
                came.wait_recv()
        if number < rounds:
            for sent, _ in passes(number):
                sent.start()

    def shared_step(b, carry):
        for number in range(rounds):
            pl.when(b == 2 * number)(lambda number=number: exchange(number))
        numerator = shared_band(b, block_ref, z_all, lead, own_tiles, pair)
        for c in range(OWN):
            sums[b, c] = numerator[:, c * BLOCK : (c + 1) * BLOCK]
        pltpu.make_async_copy(sums.at[b], sum_out.at[b], out_sem.at[0]).start()
        return carry

    lax.fori_loop(0, BANDS, shared_step, 0)
    exchange(rounds)
    degree_copy = pltpu.make_async_copy(degrees, degree_out, out_sem.at[2])
    degree_copy.start()
    pltpu.make_async_copy(sums, sum_out, out_sem.at[0]).wait()
    link_copy.wait()
    degree_copy.wait()
    drain(piece_send, 0, sent_rows)
    drain(core_send, 0, HALF)


def divide(spot_ref, sum_ref, link_ref, degree_ref, out_ref):
    b = pl.program_id(0)
    first = spot_ref[BANDS * OWN] + b
    own_row = degree_ref[pl.ds(first, 1), :]
    own = jnp.transpose(jnp.broadcast_to(own_row, (BLOCK, BLOCK)))
    for c in range(OWN):
        near = degree_ref[pl.ds(spot_ref[b * OWN + c], 1), :]
        link = link_ref[:, c * BLOCK : (c + 1) * BLOCK].astype(jnp.float32)
        out_ref[0, c] = sum_ref[0, c] / (jnp.minimum(own, near) + 1.0 - link)


def per_device(expression, nbr_owner, nbr_slot):
    row = lax.axis_index("rows")
    plane = lax.axis_index("nbr")
    owner = lax.dynamic_slice_in_dim(nbr_owner, row * BANDS, BANDS, 1)
    slot = lax.dynamic_slice_in_dim(nbr_slot, row * BANDS, BANDS, 1)

    def own_first(part):
        turned = jnp.stack([lax.dynamic_index_in_dim(part, (plane + i) % XS, 0, False) for i in range(XS)])
        return jnp.transpose(turned, (1, 0, 2)).reshape(BANDS, LIST)

    owner, slot = own_first(owner), own_first(slot)
    core, chip = owner % 2, owner // 2
    block = core * (CHIPS * BANDS) + chip * BANDS + slot
    ids = owner * BANDS + slot
    same = ids == (row * BANDS + jnp.arange(BANDS, dtype=jnp.int32))[:, None]
    position = jnp.arange(LIST, dtype=jnp.int32)
    earlier = position[None, :] < position[:, None]
    repeated = jnp.any((ids[:, :, None] == ids[:, None, :]) & earlier[None], axis=2)
    weights = (~same & ~repeated).astype(jnp.float32)
    spot = core * (CHIPS * BANDS) + (chip % YS) * (ZS * BANDS) + chip // YS * BANDS + slot
    my_chip = row // 2
    first = (row % 2) * (CHIPS * BANDS) + (my_chip % YS) * (ZS * BANDS) + my_chip // YS * BANDS
    spots = jnp.concatenate([spot[:, :OWN].reshape(-1), first[None]])

    sums, link, degrees = pl.pallas_call(
        kernel,
        out_shape=(
            jax.ShapeDtypeStruct((BANDS, OWN, BLOCK, BLOCK), jnp.float32),
            jax.ShapeDtypeStruct((SHARD, OWN_WIDTH), jnp.bfloat16),
            jax.ShapeDtypeStruct((2 * CHIPS * BANDS, BLOCK), jnp.float32),
        ),
        in_specs=[pl.BlockSpec(memory_space=pltpu.VMEM)]
        + [pl.BlockSpec(memory_space=pltpu.SMEM)] * 3,
        out_specs=(pl.BlockSpec(memory_space=pl.ANY),) * 3,
        scratch_shapes=[
            pltpu.VMEM((2 * HALF, BLOCK), jnp.bfloat16),
            pltpu.VMEM((SHARD, WIDTH), jnp.bfloat16),
            pltpu.VMEM((SHARD, OWN_WIDTH), jnp.bfloat16),
            pltpu.VMEM((BANDS, OWN, BLOCK, BLOCK), jnp.float32),
            pltpu.VMEM((2 * CHIPS * BANDS, BLOCK), jnp.float32),
            pltpu.VMEM((WIDTH, OWN_WIDTH), jnp.bfloat16),
            pltpu.SemaphoreType.DMA((len(PLAN),)),
            pltpu.SemaphoreType.DMA,
            pltpu.SemaphoreType.DMA,
            pltpu.SemaphoreType.DMA,
            pltpu.SemaphoreType.DMA((13,)),
            pltpu.SemaphoreType.DMA((13,)),
            pltpu.SemaphoreType.DMA((3,)),
        ],
        compiler_params=pltpu.CompilerParams(
            collective_id=0, has_side_effects=True, vmem_limit_bytes=60 * 2**20
        ),
    )(expression, block, weights, same[:, :OWN].astype(jnp.float32))

    return pl.pallas_call(
        divide,
        out_shape=jax.ShapeDtypeStruct((BANDS, OWN, BLOCK, BLOCK), jnp.float32),
        grid_spec=pltpu.PrefetchScalarGridSpec(
            num_scalar_prefetch=1,
            grid=(BANDS,),
            in_specs=[
                pl.BlockSpec((1, OWN, BLOCK, BLOCK), lambda b, _: (b, 0, 0, 0)),
                pl.BlockSpec((BLOCK, OWN_WIDTH), lambda b, _: (b, 0)),
                pl.BlockSpec((2 * CHIPS * BANDS, BLOCK), lambda b, _: (0, 0)),
            ],
            out_specs=pl.BlockSpec((1, OWN, BLOCK, BLOCK), lambda b, _: (b, 0, 0, 0)),
        ),
    )(spots, sums, link, degrees)


def solution(mesh):
    return jax.shard_map(
        per_device,
        mesh=mesh,
        in_specs=(P("rows", None, None), P(), P()),
        out_specs=P("rows", "nbr", None, None),
        check_vma=False,
    )
```

time: 809 us -> 133 us (0.16)
  waiting for transfers between devices: 511 us -> 0 us
  local copies, waits for them, and re-layouts: 141 us -> 1.12 us
  Pallas kernels: 0 us -> 128 us
  matrix products: 65 us -> 0 us
  other arithmetic: 46.1 us -> 3.03 us
  starting transfers between devices: 28.6 us -> 0 us
  between operations: 14.6 us -> 0.03 us
    all_to_all x2 -> x0, waiting for transfers between devices: 369 us -> none  [the longest x1 359 us: per_device(): lax.all_to_all(jnp.concatenate(outgoing, axis=1), 'rows', split_axis=0, c...]
    unnamed x2 -> x0, waiting for transfers between devices: 142 us -> none
    pallas_call x0 -> x2, Pallas kernels: none -> 128 us  [the longest x1 116 us: per_device(): pl.pallas_call(kernel, out_shape=(jax.ShapeDtypeStruct((BANDS, OWN, BLOCK...]
    dot_general x50 -> x0, matrix products: 65 us -> none  [the longest x16 43.3 us: adjacency(): jnp.einsum('uvs,cjs->uvcj', left_rows, right_rows, preferred_element_type...]
    gather x10 -> x0, local copies, waits for them, and re-layouts: 43.9 us -> none  [the longest x4 30.4 us: per_device(): flat_rows[spot_index].reshape(band_count, per_group, block_rows, samples)]
    all_to_all x2 -> x0, starting transfers between devices: 28.4 us -> none  [the longest x1 15 us: per_device(): lax.all_to_all(degree_send.astype(jnp.bfloat16), 'rows', split_axis=0, co...]
    convert_element_type x42 -> x0, local copies, waits for them, and re-layouts: 25.4 us -> none  [the longest x16 21.7 us: adjacency(): return jnp.where(zeroed, 0.0, soft_value).astype(jnp.bfloat16)]
    dynamic_slice x35 -> x1, local copies, waits for them, and re-layouts: 22.9 us -> 0.89 us  [own_first(): lax.dynamic_index_in_dim(part, (plane + i) % XS, 0, False)]
  transfers between devices with their start and end apart: 3 -> 0, of which waited for: 3 -> 0; matrix products, arithmetic and copies ran while one was open for 1% -> 0% of each run, Pallas kernels for 0% -> 0%
where the time goes in v1:
time: 133 us; the launch traced here: 132 us
  Pallas kernels  128 us (96%)
  other arithmetic  3.03 us (2%)
    pallas_call x1, Pallas kernels, per_device(): pl.pallas_call(kernel, out_shape=(jax.ShapeDtypeStruct((BANDS, OWN, BLOCK...  116 us
    pallas_call x1, Pallas kernels, per_device(): pl.pallas_call(divide, out_shape=jax.ShapeDtypeStruct((BANDS, OWN, BLOCK,...  12.2 us

profile of v1, /device:TPU:1, one launch (start us, length us, event | category | flops | bytes accessed | tf_op | source)
XLA Modules:
  0.0 132.0 jit_solution(282390884353000831)
XLA Ops:
  0.0 0.9 constant_dynamic-slice_fusion.3
  0.9 0.1 copy.18
  1.0 0.1 copy.14
  1.1 0.6 add_add_fusion
  1.7 0.4 and_reduce_fusion
  2.1 0.7 and_convert_fusion
  2.8 0.6 slice_convert_fusion.same_ref
  3.4 0.1 reshape.47
  3.5 0.7 pad_add_fusion.2.spot_ref
  4.2 115.6 %shard_map.37 = (f32[16,4,128,128]{3,2,1,0:T(8,128)}, bf16[2048,512]{1,0:T(8,128)(2,1)}, f32[1024,128]{1,0:T(8,128)}) custom-call(bf16[16,128,128]{2,1,0:T(8,128)(2,1)} %x_ref.1, s32[16,16]{1,0:T(8,128)} %get-tuple-element.13.block_ref, f32[16,16]{1,0:T(8,128)} %get-tuple-element.11.weight_ref, f32[16,4]{1,0:T(8,128)} %slice_convert_fusion.same_ref), custom_call_target="tpu_custom_call" | custom-call | tf_op jit(solution)/shard_map/pallas_call | solution.py:353
  119.8 12.2 %shard_map.38 = f32[16,4,128,128]{3,2,1,0:T(8,128)} custom-call(s32[65]{0:T(128)} %pad_add_fusion.2.spot_ref, f32[16,4,128,128]{3,2,1,0:T(8,128)} %get-tuple-element.8.sum_ref, bf16[2048,512]{1,0:T(8,128)(2,1)} %get-tuple-element.9.link_ref, f32[1024,128]{1,0:T(8,128)} %get-tuple-element.10.degree_ref), custom_call_target="tpu_custom_call" | custom-call | tf_op jit(solution)/shard_map/pallas_call | solution.py:383
  (7 shorter events, 0.1 us)

commit v2 on v1

v2 whole, which is shorter than its diff:
```python
import heapq

import jax
import jax.numpy as jnp
from jax import lax
from jax.experimental import pallas as pl
from jax.experimental.pallas import tpu as pltpu
from jax.sharding import PartitionSpec as P

MESH = pl.DeviceIdType.MESH
BLOCK = 128
BANDS = 16
LIST = 16
OWN = 4
ZS, YS, XS = 8, 4, 4
CHIPS = ZS * YS
SHARD = BANDS * BLOCK
HALF = CHIPS * SHARD
PIECE = {"A": 640, "B": 704}
START = {"A": 0, "B": 640, "C": 640 + 704}
WIDTH = LIST * BLOCK + BLOCK
OWN_WIDTH = OWN * BLOCK
NT = (((1,), (1,)), ((), ()))


def piece_rows(kind):
    return PIECE["A" if kind == "A" else "B"] // 2


def next_sends(kind, part, dy, dz):
    sends = []
    if kind == "C":
        return sends
    along_z, along_y = [], []
    if 0 <= dz < 3:
        along_z.append(("z+", kind, part, dy, dz + 1))
    if dz == 3 and part == "a":
        along_z.append(("z+", kind, part, dy, 4))
    if -3 < dz <= 0:
        along_z.append(("z-", kind, part, dy, dz - 1))
    if dz == -3 and part == "b":
        along_z.append(("z-", kind, part, dy, -4))
    if dy == 0:
        along_y += [("y+", kind, part, 1, dz), ("y-", kind, part, -1, dz)]
    if dy == 1 and part == "a":
        along_y.append(("y+", kind, part, 2, dz))
    if dy == -1 and part == "b":
        along_y.append(("y-", kind, part, -2, dz))
    if kind == "A":
        sends += along_y if dz == 0 else []
        sends += along_z
    else:
        sends += along_z if dy == 0 else []
        sends += along_y
        if dy or dz:
            sends.append(("x+" if dz % 2 == 0 else "x-", "C", part, dy, dz))
    return sends


def gather_plan():
    free, heap, order, count, clock = {}, [], [], 0, 0.0
    for kind, part in (("B", "a"), ("B", "b"), ("A", "a"), ("A", "b")):
        heapq.heappush(heap, (0.0, count, (None, kind, part, 0, 0)))
        count += 1
    while heap:
        time, _, event = heapq.heappop(heap)
        order.append(event)
        clock = max(clock, time) + 0.1
        for send in next_sends(*event[1:]):
            began = max(free.get(send[0], 0.0), clock)
            free[send[0]] = began + 2 * piece_rows(send[1]) * 256 / 95e3
            heapq.heappush(heap, (free[send[0]] + 3.2, count, send))
            count += 1
    return order


PLAN = gather_plan()
ARRIVALS = {event: number for number, event in enumerate(PLAN)}


def standardize_into(x_ref, z_all, mine):
    def one(i, carry):
        values = x_ref[i].astype(jnp.float32)
        centred = values - jnp.mean(values, axis=-1, keepdims=True)
        inverse = lax.rsqrt(jnp.sum(centred * centred, axis=-1, keepdims=True) + 1e-06)
        z_all[pl.ds(pl.multiple_of(mine + i * BLOCK, BLOCK), BLOCK), :] = (centred * inverse).astype(
            jnp.bfloat16
        )
        return carry

    lax.fori_loop(0, BANDS, one, 0)


def off_diagonal(dtype):
    i = lax.broadcasted_iota(jnp.int32, (BLOCK, BLOCK), 0)
    j = lax.broadcasted_iota(jnp.int32, (BLOCK, BLOCK), 1)
    return jnp.where(i == j, 0.0, 1.0).astype(dtype)


def block_of(z_all, block):
    return z_all[pl.ds(block * BLOCK, BLOCK), :]


def lead_band(b, my_block, block_ref, weight_ref, same_ref, z_all, lead, own_tiles):
    band = block_of(z_all, my_block + b)
    left = band * jnp.bfloat16(0.5)
    at = pl.ds(pl.multiple_of(b * BLOCK, BLOCK), BLOCK)
    apart = off_diagonal(jnp.float32)
    total = jnp.zeros((BLOCK, BLOCK), jnp.float32)
    for begin, end in ((0, 5), (5, 9), (9, 13), (13, 17)):
        right = [
            band if u == 0 else block_of(z_all, block_ref[b, u - 1]) for u in range(begin, end)
        ]
        base = 0.5 + lax.dot_general(
            left, jnp.concatenate(right, axis=0), NT, preferred_element_type=jnp.float32
        )
        second = base * base
        fourth = second * second
        soft = fourth * fourth * fourth
        for u in range(begin, end):
            tile = soft[:, (u - begin) * BLOCK : (u - begin + 1) * BLOCK]
            if u == 0:
                tile = tile * apart
            else:
                if u <= OWN:
                    tile = tile * (1.0 - same_ref[b, u - 1] * (1.0 - apart))
                    own_tiles[at, (u - 1) * BLOCK : u * BLOCK] = tile.astype(jnp.bfloat16)
                tile = tile * weight_ref[b, u - 1]
            lead[at, u * BLOCK : (u + 1) * BLOCK] = tile.astype(jnp.bfloat16)
            total = total + tile
    return jnp.sum(jnp.transpose(total), axis=0, keepdims=True)


def fill_pair(b, block_ref, z_all, own_tiles, pair):
    at = pl.ds(pl.multiple_of(b * BLOCK, BLOCK), BLOCK)
    own = [block_of(z_all, block_ref[b, c]) for c in range(OWN)]
    right = jnp.concatenate(own, axis=0) * jnp.bfloat16(0.5)
    apart = off_diagonal(jnp.bfloat16)
    pair[0:BLOCK, :] = own_tiles[at, :]
    for u in range(0, LIST, OWN):
        left = jnp.concatenate([block_of(z_all, block_ref[b, u + i]) for i in range(OWN)], axis=0)
        base = 0.5 + lax.dot_general(left, right, NT, preferred_element_type=jnp.float32)
        second = base * base
        fourth = (second * second).astype(jnp.bfloat16)
        soft = fourth * fourth * fourth
        top = (u + 1) * BLOCK
        pair[top : top + OWN * BLOCK, :] = soft
        if u == 0:
            for c in range(OWN):
                tile = slice(c * BLOCK, (c + 1) * BLOCK)
                pair[top + c * BLOCK : top + (c + 1) * BLOCK, tile] = soft[tile, tile] * apart


def sum_band(b, lead, own_tiles, sums, pair):
    at = pl.ds(pl.multiple_of(b * BLOCK, BLOCK), BLOCK)
    shared = jnp.dot(lead[at, :], pair[...], preferred_element_type=jnp.float32)
    numerator = shared + own_tiles[at, :].astype(jnp.float32)
    for c in range(OWN):
        sums[b, c] = numerator[:, c * BLOCK : (c + 1) * BLOCK]


def divide_band(b, my_degrees, spot_ref, degrees, own_tiles, sums):
    at = pl.ds(pl.multiple_of(b * BLOCK, BLOCK), BLOCK)
    own_row = degrees[pl.ds(my_degrees + b, 1), :]
    own = jnp.transpose(jnp.broadcast_to(own_row, (BLOCK, BLOCK)))
    for c in range(OWN):
        near = degrees[pl.ds(spot_ref[b, c], 1), :]
        link = own_tiles[at, c * BLOCK : (c + 1) * BLOCK].astype(jnp.float32)
        sums[b, c] = sums[b, c] / (jnp.minimum(own, near) + 1.0 - link)


def kernel(
    x_ref, block_ref, weight_ref, same_ref, spot_ref,
    out_ref,
    z_all, lead, own_tiles, sums, degrees, pair, later_pair,
    piece_recv, piece_send, core_recv, core_send, degree_recv, degree_send, out_sem,
):
    row = lax.axis_index("rows")
    plane = lax.axis_index("nbr")
    core, chip = row % 2, row // 2
    y, z = chip % YS, chip // YS
    odd = plane % 2

    def device(to_z, to_y):
        return (((to_z + ZS) % ZS * YS + (to_y + YS) % YS) * 2 + core, plane)

    links = {
        "z+": device(z + 1, y), "z-": device(z - 1, y),
        "y+": device(z, y + 1), "y-": device(z, y - 1),
        "x+": (row, (plane + 1) % XS), "x-": (row, (plane + XS - 1) % XS),
    }
    other = (chip * 2 + 1 - core, plane)
    along_z = {dz: device(z + dz, y) for dz in range(1, ZS)}
    along_y = {dy: device(z, y + dy) for dy in range(1, YS)}
    barrier = pltpu.get_barrier_semaphore()
    greeted = list(along_z.values()) + list(along_y.values()) + [links["x+"], links["x-"], other]
    for neighbour in greeted:
        pl.semaphore_signal(barrier, inc=1, device_id=neighbour, device_id_type=MESH)
    mine = core * HALF + chip * SHARD
    standardize_into(x_ref, z_all, mine)
    pl.semaphore_wait(barrier, len(greeted))

    starts = {
        "A": START["A"],
        "B": START["B"] + odd * (START["C"] - START["B"]),
        "C": START["C"] - odd * (START["C"] - START["B"]),
    }

    def rows_at(kind, part, dy, dz):
        owner = (z - dz + ZS) % ZS * YS + (y - dy + YS) % YS
        rows = piece_rows(kind)
        first = core * HALF + owner * SHARD + starts[kind] + (rows if part == "b" else 0)
        return z_all.at[pl.ds(pl.multiple_of(first, 16), rows)]

    def copy(ref, send, recv, to):
        return pltpu.make_async_remote_copy(
            src_ref=ref, dst_ref=ref, send_sem=send, recv_sem=recv, device_id=to, device_id_type=MESH
        )

    shard = z_all.at[pl.ds(pl.multiple_of(mine, SHARD), SHARD)]
    sent_rows = 0
    for event in PLAN:
        link, kind, part, dy, dz = event
        ref = rows_at(kind, part, dy, dz)
        if link is not None:
            copy(ref, piece_send, piece_recv.at[ARRIVALS[event]], links[link]).wait_recv()
        for send in next_sends(kind, part, dy, dz):
            sent_rows += piece_rows(kind)
            copy(ref, piece_send, piece_recv.at[ARRIVALS[send]], links[send[0]]).start()
        if link is not None:
            copy(ref, core_send, core_recv, other).start()
        elif kind == "A" and part == "b":
            copy(shard, core_send, core_recv, other).start()

    def drain(sem, first, rows):
        ref = z_all.at[pl.ds(first, rows)]
        pltpu.make_async_copy(ref, ref, sem).wait()

    drain(core_recv, pl.multiple_of((1 - core) * HALF, HALF), HALF)

    column = core * (CHIPS * BANDS) + y * (ZS * BANDS)
    my_degrees = column + z * BANDS

    def lead_step(step, carry):
        for i in range(4):
            b = 4 * step + i
            degrees[pl.ds(my_degrees + b, 1), :] = lead_band(
                b, mine // BLOCK, block_ref, weight_ref, same_ref, z_all, lead, own_tiles
            )
        return carry

    lax.fori_loop(0, BANDS // 4, lead_step, 0)

    def of_device(dz):
        return degrees.at[pl.ds(pl.multiple_of(column + (z - dz + ZS) % ZS * BANDS, BANDS), BANDS)]

    def of_column(dy):
        first = core * (CHIPS * BANDS) + (y - dy + YS) % YS * (ZS * BANDS)
        return degrees.at[pl.ds(pl.multiple_of(first, ZS * BANDS), ZS * BANDS)]

    def of_core(which):
        return degrees.at[pl.ds(pl.multiple_of(which * (CHIPS * BANDS), CHIPS * BANDS), CHIPS * BANDS)]

    def passed(number, ref, to):
        return copy(ref, degree_send.at[number], degree_recv.at[number], to)

    def exchange(stage):
        if stage == 1:
            for dz in range(1, ZS):
                passed(dz, of_device(dz), along_z[dz]).wait()
        if stage == 2:
            for dy in range(1, YS):
                passed(ZS + dy, of_column(dy), along_y[dy]).wait()
        if stage == 3:
            passed(0, of_core(1 - core), other).wait()
        if stage == 0:
            for dz in range(1, ZS):
                passed(dz, of_device(0), along_z[dz]).start()
        if stage == 1:
            for dy in range(1, YS):
                passed(ZS + dy, of_column(0), along_y[dy]).start()
        if stage == 2:
            passed(0, of_core(core), other).start()

    fill_pair(0, block_ref, z_all, own_tiles, pair)

    def sum_step(step, carry):
        for stage in range(3):
            pl.when(step == 2 * stage)(lambda stage=stage: exchange(stage))
        b = 2 * step
        fill_pair(b + 1, block_ref, z_all, own_tiles, later_pair)
        sum_band(b, lead, own_tiles, sums, pair)
        fill_pair(b + 2, block_ref, z_all, own_tiles, pair)
        sum_band(b + 1, lead, own_tiles, sums, later_pair)
        return carry

    lax.fori_loop(0, BANDS // 2 - 1, sum_step, 0)
    fill_pair(BANDS - 1, block_ref, z_all, own_tiles, later_pair)
    sum_band(BANDS - 2, lead, own_tiles, sums, pair)
    sum_band(BANDS - 1, lead, own_tiles, sums, later_pair)
    exchange(3)

    def divide_step(step, carry):
        for i in range(2):
            divide_band(2 * step + i, my_degrees, spot_ref, degrees, own_tiles, sums)
        two = pl.ds(2 * step, 2)
        pltpu.make_async_copy(sums.at[two], out_ref.at[two], out_sem).start()
        return carry

    lax.fori_loop(0, BANDS // 2, divide_step, 0)
    pltpu.make_async_copy(sums, out_ref, out_sem).wait()
    drain(piece_send, 0, sent_rows)
    drain(core_send, 0, HALF)


def per_device(expression, nbr_owner, nbr_slot):
    row = lax.axis_index("rows")
    plane = lax.axis_index("nbr")
    owner = lax.dynamic_slice_in_dim(nbr_owner, row * BANDS, BANDS, 1)
    slot = lax.dynamic_slice_in_dim(nbr_slot, row * BANDS, BANDS, 1)

    def own_first(part):
        turned = jnp.stack([lax.dynamic_index_in_dim(part, (plane + i) % XS, 0, False) for i in range(XS)])
        return jnp.transpose(turned, (1, 0, 2)).reshape(BANDS, LIST)

    owner, slot = own_first(owner), own_first(slot)
    core, chip = owner % 2, owner // 2
    block = core * (CHIPS * BANDS) + chip * BANDS + slot
    ids = owner * BANDS + slot
    same = ids == (row * BANDS + jnp.arange(BANDS, dtype=jnp.int32))[:, None]
    position = jnp.arange(LIST, dtype=jnp.int32)
    earlier = position[None, :] < position[:, None]
    repeated = jnp.any((ids[:, :, None] == ids[:, None, :]) & earlier[None], axis=2)
    weights = (~same & ~repeated).astype(jnp.float32)
    spot = core * (CHIPS * BANDS) + (chip % YS) * (ZS * BANDS) + chip // YS * BANDS + slot
    return pl.pallas_call(
        kernel,
        out_shape=jax.ShapeDtypeStruct((BANDS, OWN, BLOCK, BLOCK), jnp.float32),
        in_specs=[pl.BlockSpec(memory_space=pltpu.VMEM)]
        + [pl.BlockSpec(memory_space=pltpu.SMEM)] * 4,
        out_specs=pl.BlockSpec(memory_space=pl.ANY),
        scratch_shapes=[
            pltpu.VMEM((2 * HALF, BLOCK), jnp.bfloat16),
            pltpu.VMEM((SHARD, WIDTH), jnp.bfloat16),
            pltpu.VMEM((SHARD, OWN_WIDTH), jnp.bfloat16),
            pltpu.VMEM((BANDS, OWN, BLOCK, BLOCK), jnp.float32),
            pltpu.VMEM((2 * CHIPS * BANDS, BLOCK), jnp.float32),
            pltpu.VMEM((WIDTH, OWN_WIDTH), jnp.bfloat16),
            pltpu.VMEM((WIDTH, OWN_WIDTH), jnp.bfloat16),
            pltpu.SemaphoreType.DMA((len(PLAN),)),
            pltpu.SemaphoreType.DMA,
            pltpu.SemaphoreType.DMA,
            pltpu.SemaphoreType.DMA,
            pltpu.SemaphoreType.DMA((ZS + YS,)),
            pltpu.SemaphoreType.DMA((ZS + YS,)),
            pltpu.SemaphoreType.DMA,
        ],
        compiler_params=pltpu.CompilerParams(
            collective_id=0, has_side_effects=True, vmem_limit_bytes=60 * 2**20
        ),
    )(expression, block, weights, same[:, :OWN].astype(jnp.float32), spot[:, :OWN])


def solution(mesh):
    return jax.shard_map(
        per_device,
        mesh=mesh,
        in_specs=(P("rows", None, None), P(), P()),
        out_specs=P("rows", "nbr", None, None),
        check_vma=False,
    )
```

time: 133 us -> 118 us (0.89)
  Pallas kernels: 128 us -> 109 us
  local copies, waits for them, and re-layouts: 1.12 us -> 5.74 us
    pallas_call x2 -> x1, Pallas kernels: 128 us -> 109 us  [per_device(): pl.pallas_call(kernel, out_shape=jax.ShapeDtypeStruct((BANDS, OWN, BLOCK,...]
    unnamed x0 -> x1, local copies, waits for them, and re-layouts: none -> 4.7 us
where the time goes in v2:
time: 118 us
  Pallas kernels  109 us (92%)
  local copies, waits for them, and re-layouts  5.74 us (5%)
  other arithmetic  2.97 us (3%)
    pallas_call x1, Pallas kernels, per_device(): pl.pallas_call(kernel, out_shape=jax.ShapeDtypeStruct((BANDS, OWN, BLOCK,...  109 us
    unnamed x1, local copies, waits for them, and re-layouts  4.7 us

profile of v2, /device:TPU:1, one launch (start us, length us, event | category | flops | bytes accessed | tf_op | source)
XLA Modules:
  0.0 117.7 jit_solution(14253688997676448974)
XLA Ops:
  0.0 0.9 constant_dynamic-slice_fusion.3
  0.9 0.1 copy.18
  1.0 0.1 copy.14
  1.1 0.6 multiply_add_fusion
  1.7 0.4 and_reduce_fusion
  2.2 0.6 fusion.4.spot_ref
  2.8 0.7 and_convert_fusion
  3.4 0.6 slice_convert_fusion.same_ref
  4.0 109.0 %shard_map.37 = f32[16,4,128,128]{3,2,1,0:T(8,128)} custom-call(bf16[16,128,128]{2,1,0:T(8,128)(2,1)} %x_ref.1, s32[16,16]{1,0:T(8,128)} %get-tuple-element.18.block_ref, f32[16,16]{1,0:T(8,128)} %get-tuple-element.7.weight_ref, f32[16,4]{1,0:T(8,128)} %slice_convert_fusion.same_ref, s32[16,4]{1,0:T(8,128)} %fusion.4.spot_ref), custom_call_target="tpu_custom_call" | custom-call | tf_op jit(solution)/shard_map/pallas_call | solution.py:336
  113.0 4.7 %copy.23 = f32[16,4,128,128]{3,2,1,0:T(8,128)} copy(f32[16,4,128,128]{3,2,1,0:T(8,128)} %shard_map.37) | data formatting | bytes 8388608
  (6 shorter events, 0.1 us)

commit v3 on v2

v3 whole, which is shorter than its diff:
```python
import heapq

import jax
import jax.numpy as jnp
from jax import lax
from jax.experimental import pallas as pl
from jax.experimental.pallas import tpu as pltpu
from jax.sharding import PartitionSpec as P

MESH = pl.DeviceIdType.MESH
BLOCK = 128
BANDS = 16
LIST = 16
OWN = 4
ZS, YS, XS = 8, 4, 4
CHIPS = ZS * YS
SHARD = BANDS * BLOCK
HALF = CHIPS * SHARD
ROWS = {("A", "a"): 272, ("A", "b"): 272, ("B", "a"): 416, ("B", "b"): 416, ("C", "a"): 416, ("C", "b"): 256}
EVEN = {("A", "a"): 0, ("A", "b"): 272, ("B", "a"): 544, ("B", "b"): 960, ("C", "a"): 544, ("C", "b"): 960}
ODD = {("A", "a"): 0, ("A", "b"): 272, ("B", "a"): 1632, ("B", "b"): 1216, ("C", "a"): 1632, ("C", "b"): 1376}
WIDTH = LIST * BLOCK + BLOCK
OWN_WIDTH = OWN * BLOCK
NT = (((1,), (1,)), ((), ()))


def next_sends(kind, part, dy, dz):
    sends = []
    if kind == "C":
        return sends
    along_z, along_y = [], []
    if 0 <= dz < 3:
        along_z.append(("z+", kind, part, dy, dz + 1))
    if dz == 3 and part == "a":
        along_z.append(("z+", kind, part, dy, 4))
    if -3 < dz <= 0:
        along_z.append(("z-", kind, part, dy, dz - 1))
    if dz == -3 and part == "b":
        along_z.append(("z-", kind, part, dy, -4))
    if dy == 0:
        along_y += [("y+", kind, part, 1, dz), ("y-", kind, part, -1, dz)]
    if dy == 1 and part == "a":
        along_y.append(("y+", kind, part, 2, dz))
    if dy == -1 and part == "b":
        along_y.append(("y-", kind, part, -2, dz))
    if kind == "A":
        sends += along_y if dz == 0 else []
        sends += along_z
    else:
        sends += along_z if dy == 0 else []
        sends += along_y
        if dy or dz:
            sends.append(("x+" if dz % 2 == 0 else "x-", "C", part, dy, dz))
    return sends


def gather_plan():
    free, heap, order, count, clock = {}, [], [], 0, 0.0
    for kind, part in (("B", "a"), ("B", "b"), ("A", "a"), ("A", "b")):
        heapq.heappush(heap, (0.0, count, (None, kind, part, 0, 0)))
        count += 1
    while heap:
        time, _, event = heapq.heappop(heap)
        order.append(event)
        clock = max(clock, time) + 0.1
        for send in next_sends(*event[1:]):
            began = max(free.get(send[0], 0.0), clock)
            free[send[0]] = began + 2 * ROWS[send[1:3]] * 256 / 95e3
            heapq.heappush(heap, (free[send[0]] + 3.2, count, send))
            count += 1
    return order


PLAN = gather_plan()
ARRIVALS = {event: number for number, event in enumerate(PLAN)}


def standardize_into(x_ref, z_all, mine):
    def four(step, carry):
        for i in range(4):
            block = 4 * step + i
            values = x_ref[block].astype(jnp.float32)
            centred = values - jnp.mean(values, axis=-1, keepdims=True)
            inverse = lax.rsqrt(jnp.sum(centred * centred, axis=-1, keepdims=True) + 1e-06)
            rows = pl.ds(pl.multiple_of(mine + block * BLOCK, BLOCK), BLOCK)
            z_all[rows, :] = (centred * inverse).astype(jnp.bfloat16)
        return carry

    lax.fori_loop(0, BANDS // 4, four, 0)


def list_blocks(row, plane, lists, blocks, weights):
    groups = [(plane + i) % XS for i in range(XS)]
    owner = jnp.concatenate([lists[0, group] for group in groups], axis=0)
    slot = jnp.concatenate([lists[1, group] for group in groups], axis=0)
    block = (owner & 1) * (CHIPS * BANDS) + (owner >> 1) * BANDS + slot
    lane = lax.broadcasted_iota(jnp.int32, (LIST, BLOCK), 1)
    place = lax.broadcasted_iota(jnp.int32, (LIST, BLOCK), 0)
    band_row = row // 8 * 8 + (lane >> 4)
    band = (band_row & 1) * (CHIPS * BANDS) + (band_row >> 1) * BANDS + (lane & 15)
    kept = jnp.where(block == band, 0.0, 1.0)
    for earlier in range(LIST - 1):
        repeats = (block == block[earlier : earlier + 1]) & (place > earlier)
        kept = jnp.where(repeats, 0.0, kept)
    blocks[...] = block
    weights[...] = kept


def off_diagonal(dtype):
    i = lax.broadcasted_iota(jnp.int32, (BLOCK, BLOCK), 0)
    j = lax.broadcasted_iota(jnp.int32, (BLOCK, BLOCK), 1)
    return jnp.where(i == j, 0.0, 1.0).astype(dtype)


def block_of(z_all, block):
    return z_all[pl.ds(block * BLOCK, BLOCK), :]


def lead_band(b, my_block, listed, weight, z_all, lead, own_tiles):
    band = block_of(z_all, my_block + b)
    left = band * jnp.bfloat16(0.5)
    at = pl.ds(pl.multiple_of(b * BLOCK, BLOCK), BLOCK)
    apart = off_diagonal(jnp.float32)
    total = jnp.zeros((BLOCK, BLOCK), jnp.float32)
    for begin, end in ((0, 5), (5, 9), (9, 13), (13, 17)):
        right = [
            band if u == 0 else block_of(z_all, listed(b, u - 1)) for u in range(begin, end)
        ]
        base = 0.5 + lax.dot_general(
            left, jnp.concatenate(right, axis=0), NT, preferred_element_type=jnp.float32
        )
        second = base * base
        fourth = second * second
        soft = fourth * fourth * fourth
        for u in range(begin, end):
            tile = soft[:, (u - begin) * BLOCK : (u - begin + 1) * BLOCK]
            if u == 0:
                tile = tile * apart
            else:
                if u <= OWN:
                    tile = tile * (1.0 - (1.0 - weight(b, u - 1)) * (1.0 - apart))
                    own_tiles[at, (u - 1) * BLOCK : u * BLOCK] = tile.astype(jnp.bfloat16)
                tile = tile * weight(b, u - 1)
            lead[at, u * BLOCK : (u + 1) * BLOCK] = tile.astype(jnp.bfloat16)
            total = total + tile
    return jnp.sum(jnp.transpose(total), axis=0, keepdims=True)


def fill_pair(b, listed, z_all, own_tiles, pair):
    at = pl.ds(pl.multiple_of(b * BLOCK, BLOCK), BLOCK)
    own = [block_of(z_all, listed(b, c)) for c in range(OWN)]
    right = jnp.concatenate(own, axis=0) * jnp.bfloat16(0.5)
    apart = off_diagonal(jnp.bfloat16)
    pair[0:BLOCK, :] = own_tiles[at, :]
    for u in range(0, LIST, OWN):
        left = jnp.concatenate([block_of(z_all, listed(b, u + i)) for i in range(OWN)], axis=0)
        base = 0.5 + lax.dot_general(left, right, NT, preferred_element_type=jnp.float32)
        second = base * base
        fourth = (second * second).astype(jnp.bfloat16)
        soft = fourth * fourth * fourth
        top = (u + 1) * BLOCK
        pair[top : top + OWN * BLOCK, :] = soft
        if u == 0:
            for c in range(OWN):
                tile = slice(c * BLOCK, (c + 1) * BLOCK)
                pair[top + c * BLOCK : top + (c + 1) * BLOCK, tile] = soft[tile, tile] * apart


def sum_band(b, lead, own_tiles, sums, pair):
    at = pl.ds(pl.multiple_of(b * BLOCK, BLOCK), BLOCK)
    shared = jnp.dot(lead[at, :], pair[...], preferred_element_type=jnp.float32)
    numerator = shared + own_tiles[at, :].astype(jnp.float32)
    for c in range(OWN):
        sums[b, c] = numerator[:, c * BLOCK : (c + 1) * BLOCK]


def divide_band(b, my_degrees, listed, degrees, own_tiles, sums):
    at = pl.ds(pl.multiple_of(b * BLOCK, BLOCK), BLOCK)
    own_row = degrees[pl.ds(my_degrees + b, 1), :]
    own = jnp.transpose(jnp.broadcast_to(own_row, (BLOCK, BLOCK)))
    for c in range(OWN):
        near = degrees[pl.ds(listed(b, c), 1), :]
        link = own_tiles[at, c * BLOCK : (c + 1) * BLOCK].astype(jnp.float32)
        sums[b, c] = sums[b, c] / (jnp.minimum(own, near) + 1.0 - link)


def kernel(
    x_ref, owner_ref, slot_ref,
    out_ref,
    lists, blocks, weights, block_ref, weight_ref,
    z_all, lead, own_tiles, sums, degrees, pair, later_pair,
    piece_recv, piece_send, core_recv, core_send, degree_recv, degree_send, out_sem, list_sem,
):
    row = lax.axis_index("rows")
    plane = lax.axis_index("nbr")
    core, chip = row % 2, row // 2
    y, z = chip % YS, chip // YS
    odd = plane % 2

    def device(to_z, to_y):
        return (((to_z + ZS) % ZS * YS + (to_y + YS) % YS) * 2 + core, plane)

    links = {
        "z+": device(z + 1, y), "z-": device(z - 1, y),
        "y+": device(z, y + 1), "y-": device(z, y - 1),
        "x+": (row, (plane + 1) % XS), "x-": (row, (plane + XS - 1) % XS),
    }
    other = (chip * 2 + 1 - core, plane)
    along_z = {dz: device(z + dz, y) for dz in range(1, ZS)}
    along_y = {dy: device(z, y + dy) for dy in range(1, YS)}
    barrier = pltpu.get_barrier_semaphore()
    greeted = list(along_z.values()) + list(along_y.values()) + [links["x+"], links["x-"], other]
    for neighbour in greeted:
        pl.semaphore_signal(barrier, inc=1, device_id=neighbour, device_id_type=MESH)
    window = pl.ds(pl.multiple_of(row // 8 * BLOCK, BLOCK), BLOCK)
    list_copies = [
        pltpu.make_async_copy(ref.at[:, :, window], lists.at[i], list_sem.at[i])
        for i, ref in enumerate((owner_ref, slot_ref))
    ]
    for list_copy in list_copies:
        list_copy.start()
    mine = core * HALF + chip * SHARD
    standardize_into(x_ref, z_all, mine)
    pl.semaphore_wait(barrier, len(greeted))

    def rows_at(kind, part, dy, dz, parity):
        owner = (z - dz + ZS) % ZS * YS + (y - dy + YS) % YS
        first = core * HALF + owner * SHARD + EVEN[kind, part]
        apart = ODD[kind, part] - EVEN[kind, part]
        if apart:
            first = first + parity * apart
        return z_all.at[pl.ds(pl.multiple_of(first, 16), ROWS[kind, part])]

    def copy(ref, send, recv, to):
        return pltpu.make_async_remote_copy(
            src_ref=ref, dst_ref=ref, send_sem=send, recv_sem=recv, device_id=to, device_id_type=MESH
        )

    shard = z_all.at[pl.ds(pl.multiple_of(mine, SHARD), SHARD)]
    sent_rows = 0
    for number, event in enumerate(PLAN):
        link, kind, part, dy, dz = event
        ref = rows_at(kind, part, dy, dz, 1 - odd if kind == "C" else odd)
        if number == 4:
            for list_copy in list_copies:
                list_copy.wait()
            list_blocks(row, plane, lists, blocks, weights)
            number_copies = [
                pltpu.make_async_copy(blocks, block_ref, list_sem.at[0]),
                pltpu.make_async_copy(weights, weight_ref, list_sem.at[1]),
            ]
            for number_copy in number_copies:
                number_copy.start()
        if link is not None:
            copy(ref, piece_send, piece_recv.at[ARRIVALS[event]], links[link]).wait_recv()
        for send in next_sends(kind, part, dy, dz):
            sent_rows += ROWS[send[1:3]]
            sent = rows_at("C", part, dy, dz, odd) if send[1] == "C" else ref
            copy(sent, piece_send, piece_recv.at[ARRIVALS[send]], links[send[0]]).start()
        if link is not None:
            copy(ref, core_send, core_recv, other).start()
        elif kind == "A" and part == "b":
            copy(shard, core_send, core_recv, other).start()
    for number_copy in number_copies:
        number_copy.wait()
    first_lane = row % 8 * BANDS

    def listed(b, k):
        return block_ref[k, first_lane + b]

    def weight(b, k):
        return weight_ref[k, first_lane + b]

    def drain(sem, first, rows):
        ref = z_all.at[pl.ds(first, rows)]
        pltpu.make_async_copy(ref, ref, sem).wait()

    drain(core_recv, pl.multiple_of((1 - core) * HALF, HALF), HALF)

    my_degrees = mine // BLOCK

    def lead_step(step, carry):
        for i in range(4):
            b = 4 * step + i
            degrees[pl.ds(my_degrees + b, 1), :] = lead_band(
                b, mine // BLOCK, listed, weight, z_all, lead, own_tiles
            )
        return carry

    lax.fori_loop(0, BANDS // 4, lead_step, 0)

    def of_device(dy):
        first = core * (CHIPS * BANDS) + (z * YS + (y - dy + YS) % YS) * BANDS
        return degrees.at[pl.ds(pl.multiple_of(first, BANDS), BANDS)]

    def of_line(dz):
        first = core * (CHIPS * BANDS) + (z - dz + ZS) % ZS * (YS * BANDS)
        return degrees.at[pl.ds(pl.multiple_of(first, YS * BANDS), YS * BANDS)]

    def of_core(which):
        return degrees.at[pl.ds(pl.multiple_of(which * (CHIPS * BANDS), CHIPS * BANDS), CHIPS * BANDS)]

    def passed(number, ref, to):
        return copy(ref, degree_send.at[number], degree_recv.at[number], to)

    def exchange(stage):
        if stage == 1:
            for dy in range(1, YS):
                passed(ZS + dy, of_device(dy), along_y[dy]).wait()
        if stage == 2:
            for dz in range(1, ZS):
                passed(dz, of_line(dz), along_z[dz]).wait()
        if stage == 3:
            passed(0, of_core(1 - core), other).wait()
        if stage == 0:
            for dy in range(1, YS):
                passed(ZS + dy, of_device(0), along_y[dy]).start()
        if stage == 1:
            for dz in range(1, ZS):
                passed(dz, of_line(0), along_z[dz]).start()
        if stage == 2:
            passed(0, of_core(core), other).start()

    fill_pair(0, listed, z_all, own_tiles, pair)

    def sum_step(step, carry):
        for stage in range(3):
            pl.when(step == 2 * stage)(lambda stage=stage: exchange(stage))
        b = 2 * step
        fill_pair(b + 1, listed, z_all, own_tiles, later_pair)
        sum_band(b, lead, own_tiles, sums, pair)
        fill_pair(b + 2, listed, z_all, own_tiles, pair)
        sum_band(b + 1, lead, own_tiles, sums, later_pair)
        return carry

    lax.fori_loop(0, BANDS // 2 - 1, sum_step, 0)
    fill_pair(BANDS - 1, listed, z_all, own_tiles, later_pair)
    sum_band(BANDS - 2, lead, own_tiles, sums, pair)
    sum_band(BANDS - 1, lead, own_tiles, sums, later_pair)
    exchange(3)

    def divide_step(step, carry):
        for i in range(2):
            divide_band(2 * step + i, my_degrees, listed, degrees, own_tiles, sums)
        two = pl.ds(2 * step, 2)
        pltpu.make_async_copy(sums.at[two], out_ref.at[two], out_sem).start()
        return carry

    lax.fori_loop(0, BANDS // 2, divide_step, 0)
    pltpu.make_async_copy(sums, out_ref, out_sem).wait()
    drain(piece_send, 0, sent_rows)
    drain(core_send, 0, HALF)


def per_device(expression, nbr_owner, nbr_slot):
    return pl.pallas_call(
        kernel,
        out_shape=jax.ShapeDtypeStruct((BANDS, OWN, BLOCK, BLOCK), jnp.float32),
        in_specs=[pl.BlockSpec(memory_space=pltpu.VMEM)]
        + [pl.BlockSpec(memory_space=pl.ANY)] * 2,
        out_specs=pl.BlockSpec(memory_space=pl.ANY),
        scratch_shapes=[
            pltpu.VMEM((2, XS, OWN, BLOCK), jnp.int32),
            pltpu.VMEM((LIST, BLOCK), jnp.int32),
            pltpu.VMEM((LIST, BLOCK), jnp.float32),
            pltpu.SMEM((LIST, BLOCK), jnp.int32),
            pltpu.SMEM((LIST, BLOCK), jnp.float32),
            pltpu.VMEM((2 * HALF, BLOCK), jnp.bfloat16),
            pltpu.VMEM((SHARD, WIDTH), jnp.bfloat16),
            pltpu.VMEM((SHARD, OWN_WIDTH), jnp.bfloat16),
            pltpu.VMEM((BANDS, OWN, BLOCK, BLOCK), jnp.float32),
            pltpu.VMEM((2 * CHIPS * BANDS, BLOCK), jnp.float32),
            pltpu.VMEM((WIDTH, OWN_WIDTH), jnp.bfloat16),
            pltpu.VMEM((WIDTH, OWN_WIDTH), jnp.bfloat16),
            pltpu.SemaphoreType.DMA((len(PLAN),)),
            pltpu.SemaphoreType.DMA,
            pltpu.SemaphoreType.DMA,
            pltpu.SemaphoreType.DMA,
            pltpu.SemaphoreType.DMA((ZS + YS,)),
            pltpu.SemaphoreType.DMA((ZS + YS,)),
            pltpu.SemaphoreType.DMA,
            pltpu.SemaphoreType.DMA((2,)),
        ],
        compiler_params=pltpu.CompilerParams(
            collective_id=0, has_side_effects=True, vmem_limit_bytes=60 * 2**20
        ),
    )(expression, jnp.transpose(nbr_owner, (0, 2, 1)), jnp.transpose(nbr_slot, (0, 2, 1)))


def solution(mesh):
    return jax.shard_map(
        per_device,
        mesh=mesh,
        in_specs=(P("rows", None, None), P(), P()),
        out_specs=P("rows", "nbr", None, None),
        check_vma=False,
    )
```

time: 118 us -> 116 us (0.983)
  other arithmetic: 2.97 us -> 0 us
  Pallas kernels: 109 us -> 111 us
    pallas_call x1, Pallas kernels: 109 us -> 111 us  [per_device(): pl.pallas_call(kernel, out_shape=jax.ShapeDtypeStruct((BANDS, OWN, BLOCK,...]
    convert_element_type x2 -> x0, other arithmetic: 1.26 us -> none  [the longest x1 0.67 us: per_device(): weights = (~same & ~repeated).astype(jnp.float32)]
    add x3 -> x0, other arithmetic: 1.23 us -> none  [the longest x1 0.61 us: per_device(): core * (CHIPS * BANDS) + chip % YS * (ZS * BANDS) + chip // YS * BANDS]
where the time goes in v3:
time: 116 us
  Pallas kernels  111 us (96%)
  local copies, waits for them, and re-layouts  4.7 us (4%)
    pallas_call x1, Pallas kernels, per_device(): pl.pallas_call(kernel, out_shape=jax.ShapeDtypeStruct((BANDS, OWN, BLOCK,...  111 us
    unnamed x1, local copies, waits for them, and re-layouts  4.7 us

profile of v3, /device:TPU:1, one launch (start us, length us, event | category | flops | bytes accessed | tf_op | source)
XLA Modules:
  0.0 115.5 jit_solution(5250701736203234632)
XLA Ops:
  0.0 110.8 %shard_map.37 = f32[16,4,128,128]{3,2,1,0:T(8,128)} custom-call(bf16[16,128,128]{2,1,0:T(8,128)(2,1)} %x_ref.1, s32[4,4,1024]{2,1,0:T(4,128)} %bitcast.2, s32[4,4,1024]{2,1,0:T(4,128)} %bitcast.3), custom_call_target="tpu_custom_call" | custom-call | tf_op jit(solution)/shard_map/pallas_call | solution.py:356
  110.8 4.7 %copy.5 = f32[16,4,128,128]{3,2,1,0:T(8,128)} copy(f32[16,4,128,128]{3,2,1,0:T(8,128)} %shard_map.37) | data formatting | bytes 8388608

commit v4 on v3

--- a/solution.py
+++ b/solution.py
@@ -16,9 +16,9 @@
 CHIPS = ZS * YS
 SHARD = BANDS * BLOCK
 HALF = CHIPS * SHARD
-ROWS = {("A", "a"): 272, ("A", "b"): 272, ("B", "a"): 416, ("B", "b"): 416, ("C", "a"): 416, ("C", "b"): 256}
-EVEN = {("A", "a"): 0, ("A", "b"): 272, ("B", "a"): 544, ("B", "b"): 960, ("C", "a"): 544, ("C", "b"): 960}
-ODD = {("A", "a"): 0, ("A", "b"): 272, ("B", "a"): 1632, ("B", "b"): 1216, ("C", "a"): 1632, ("C", "b"): 1376}
+ROWS = {("A", "a"): 320, ("A", "b"): 320, ("B", "a"): 368, ("B", "b"): 368, ("C", "a"): 368, ("C", "b"): 304}
+EVEN = {("A", "a"): 0, ("A", "b"): 320, ("B", "a"): 640, ("B", "b"): 1008, ("C", "a"): 640, ("C", "b"): 1008}
+ODD = {("A", "a"): 0, ("A", "b"): 320, ("B", "a"): 1680, ("B", "b"): 1312, ("C", "a"): 1680, ("C", "b"): 1376}
 WIDTH = LIST * BLOCK + BLOCK
 OWN_WIDTH = OWN * BLOCK
 NT = (((1,), (1,)), ((), ()))
@@ -174,19 +174,18 @@
         sums[b, c] = numerator[:, c * BLOCK : (c + 1) * BLOCK]
 
 
-def divide_band(b, my_degrees, listed, degrees, own_tiles, sums):
-    at = pl.ds(pl.multiple_of(b * BLOCK, BLOCK), BLOCK)
-    own_row = degrees[pl.ds(my_degrees + b, 1), :]
-    own = jnp.transpose(jnp.broadcast_to(own_row, (BLOCK, BLOCK)))
-    for c in range(OWN):
-        near = degrees[pl.ds(listed(b, c), 1), :]
-        link = own_tiles[at, c * BLOCK : (c + 1) * BLOCK].astype(jnp.float32)
-        sums[b, c] = sums[b, c] / (jnp.minimum(own, near) + 1.0 - link)
+def divide(sum_ref, link_ref, own_ref, near_ref, out_ref):
+    for b in range(sum_ref.shape[0]):
+        own = jnp.transpose(jnp.broadcast_to(own_ref[b : b + 1, :], (BLOCK, BLOCK)))
+        for c in range(OWN):
+            tile = link_ref[b * BLOCK : (b + 1) * BLOCK, c * BLOCK : (c + 1) * BLOCK]
+            link = tile.astype(jnp.float32)
+            out_ref[b, c] = sum_ref[b, c] / (jnp.minimum(own, near_ref[b, c : c + 1, :]) + 1.0 - link)
 
 
 def kernel(
     x_ref, owner_ref, slot_ref,
-    out_ref,
+    sum_out, link_out, own_out, near_out,
     lists, blocks, weights, block_ref, weight_ref,
     z_all, lead, own_tiles, sums, degrees, pair, later_pair,
     piece_recv, piece_send, core_recv, core_send, degree_recv, degree_send, out_sem, list_sem,
@@ -288,6 +287,11 @@
         return carry
 
     lax.fori_loop(0, BANDS // 4, lead_step, 0)
+    link_copy = pltpu.make_async_copy(own_tiles, link_out, out_sem.at[1])
+    link_copy.start()
+
+    def emit(b):
+        pltpu.make_async_copy(sums.at[b], sum_out.at[b], out_sem.at[0]).start()
 
     def of_device(dy):
         first = core * (CHIPS * BANDS) + (z * YS + (y - dy + YS) % YS) * BANDS
@@ -331,34 +335,44 @@
         sum_band(b, lead, own_tiles, sums, pair)
         fill_pair(b + 2, listed, z_all, own_tiles, pair)
         sum_band(b + 1, lead, own_tiles, sums, later_pair)
+        emit(b)
+        emit(b + 1)
         return carry
 
     lax.fori_loop(0, BANDS // 2 - 1, sum_step, 0)
     fill_pair(BANDS - 1, listed, z_all, own_tiles, later_pair)
     sum_band(BANDS - 2, lead, own_tiles, sums, pair)
     sum_band(BANDS - 1, lead, own_tiles, sums, later_pair)
+    emit(BANDS - 2)
+    emit(BANDS - 1)
     exchange(3)
-
-    def divide_step(step, carry):
-        for i in range(2):
-            divide_band(2 * step + i, my_degrees, listed, degrees, own_tiles, sums)
-        two = pl.ds(2 * step, 2)
-        pltpu.make_async_copy(sums.at[two], out_ref.at[two], out_sem).start()
+    own_out[...] = degrees[pl.ds(pl.multiple_of(my_degrees, BANDS), BANDS), :]
+
+    def near_step(b, carry):
+        for c in range(OWN):
+            near_out[b, c : c + 1, :] = degrees[pl.ds(listed(b, c), 1), :]
         return carry
 
-    lax.fori_loop(0, BANDS // 2, divide_step, 0)
-    pltpu.make_async_copy(sums, out_ref, out_sem).wait()
+    lax.fori_loop(0, BANDS, near_step, 0)
+    link_copy.wait()
+    pltpu.make_async_copy(sums, sum_out, out_sem.at[0]).wait()
     drain(piece_send, 0, sent_rows)
     drain(core_send, 0, HALF)
 
 
 def per_device(expression, nbr_owner, nbr_slot):
-    return pl.pallas_call(
+    sums, links, own, near = pl.pallas_call(
         kernel,
-        out_shape=jax.ShapeDtypeStruct((BANDS, OWN, BLOCK, BLOCK), jnp.float32),
+        out_shape=(
+            jax.ShapeDtypeStruct((BANDS, OWN, BLOCK, BLOCK), jnp.float32),
+            jax.ShapeDtypeStruct((SHARD, OWN_WIDTH), jnp.bfloat16),
+            jax.ShapeDtypeStruct((BANDS, BLOCK), jnp.float32),
+            jax.ShapeDtypeStruct((BANDS, OWN, BLOCK), jnp.float32),
+        ),
         in_specs=[pl.BlockSpec(memory_space=pltpu.VMEM)]
         + [pl.BlockSpec(memory_space=pl.ANY)] * 2,
-        out_specs=pl.BlockSpec(memory_space=pl.ANY),
+        out_specs=(pl.BlockSpec(memory_space=pl.ANY),) * 2
+        + (pl.BlockSpec(memory_space=pltpu.VMEM),) * 2,
         scratch_shapes=[
             pltpu.VMEM((2, XS, OWN, BLOCK), jnp.int32),
             pltpu.VMEM((LIST, BLOCK), jnp.int32),
@@ -378,13 +392,29 @@
             pltpu.SemaphoreType.DMA,
             pltpu.SemaphoreType.DMA((ZS + YS,)),
             pltpu.SemaphoreType.DMA((ZS + YS,)),
-            pltpu.SemaphoreType.DMA,
+            pltpu.SemaphoreType.DMA((2,)),
             pltpu.SemaphoreType.DMA((2,)),
         ],
         compiler_params=pltpu.CompilerParams(
             collective_id=0, has_side_effects=True, vmem_limit_bytes=60 * 2**20
         ),
     )(expression, jnp.transpose(nbr_owner, (0, 2, 1)), jnp.transpose(nbr_slot, (0, 2, 1)))
+
+    steps = 2
+    half = BANDS // steps
+    tiles = pl.BlockSpec((half, OWN, BLOCK, BLOCK), lambda i: (i, 0, 0, 0))
+    return pl.pallas_call(
+        divide,
+        out_shape=jax.ShapeDtypeStruct((BANDS, OWN, BLOCK, BLOCK), jnp.float32),
+        grid=(steps,),
+        in_specs=[
+            tiles,
+            pl.BlockSpec((half * BLOCK, OWN_WIDTH), lambda i: (i, 0)),
+            pl.BlockSpec((half, BLOCK), lambda i: (i, 0)),
+            pl.BlockSpec((half, OWN, BLOCK), lambda i: (i, 0, 0)),
+        ],
+        out_specs=tiles,
+    )(sums, links, own, near)
 
 
 def solution(mesh):

time: 116 us -> 115 us (level)
  local copies, waits for them, and re-layouts: 4.7 us -> 0 us
  Pallas kernels: 111 us -> 115 us
    unnamed x1 -> x0, local copies, waits for them, and re-layouts: 4.7 us -> none
    pallas_call x1 -> x2, Pallas kernels: 111 us -> 115 us  [the longest x1 110 us: per_device(): pl.pallas_call(kernel, out_shape=(jax.ShapeDtypeStruct((BANDS, OWN, BLOCK...]
where the time goes in v4:
time: 115 us
  Pallas kernels  115 us (100%)
    pallas_call x1, Pallas kernels, per_device(): pl.pallas_call(kernel, out_shape=(jax.ShapeDtypeStruct((BANDS, OWN, BLOCK...  110 us
    pallas_call x1, Pallas kernels, per_device(): pl.pallas_call(divide, out_shape=jax.ShapeDtypeStruct((BANDS, OWN, BLOCK,...  4.73 us

profile of v4, /device:TPU:1, one launch (start us, length us, event | category | flops | bytes accessed | tf_op | source)
XLA Modules:
  0.0 114.7 jit_solution(3493294834567236888)
XLA Ops:
  0.0 110.0 %shard_map.37 = (f32[16,4,128,128]{3,2,1,0:T(8,128)}, bf16[2048,512]{1,0:T(8,128)(2,1)}, f32[16,128]{1,0:T(8,128)}, f32[16,4,128]{2,1,0:T(4,128)}) custom-call(bf16[16,128,128]{2,1,0:T(8,128)(2,1)} %x_ref.1, s32[4,4,1024]{2,1,0:T(4,128)} %bitcast.2, s32[4,4,1024]{2,1,0:T(4,128)} %bitcast.3), custom_call_target="tpu_custom_call" | custom-call | tf_op jit(solution)/shard_map/pallas_call | solution.py:364
  110.0 4.7 %shard_map.38 = f32[16,4,128,128]{3,2,1,0:T(8,128)} custom-call(f32[16,4,128,128]{3,2,1,0:T(8,128)} %get-tuple-element.9.sum_ref, bf16[2048,512]{1,0:T(8,128)(2,1)} %get-tuple-element.10.link_ref, f32[16,128]{1,0:T(8,128)} %get-tuple-element.11.own_ref, f32[16,4,128]{2,1,0:T(4,128)} %get-tuple-element.12.near_ref), custom_call_target="tpu_custom_call" | custom-call | tf_op jit(solution)/shard_map/pallas_call | solution.py:406

commit v5 on v4

--- a/solution.py
+++ b/solution.py
@@ -16,9 +16,9 @@
 CHIPS = ZS * YS
 SHARD = BANDS * BLOCK
 HALF = CHIPS * SHARD
-ROWS = {("A", "a"): 320, ("A", "b"): 320, ("B", "a"): 368, ("B", "b"): 368, ("C", "a"): 368, ("C", "b"): 304}
-EVEN = {("A", "a"): 0, ("A", "b"): 320, ("B", "a"): 640, ("B", "b"): 1008, ("C", "a"): 640, ("C", "b"): 1008}
-ODD = {("A", "a"): 0, ("A", "b"): 320, ("B", "a"): 1680, ("B", "b"): 1312, ("C", "a"): 1680, ("C", "b"): 1376}
+ROWS = {("A", "a"): 304, ("A", "b"): 304, ("B", "a"): 384, ("B", "b"): 384, ("C", "a"): 384, ("C", "b"): 288}
+EVEN = {("A", "a"): 0, ("A", "b"): 304, ("B", "a"): 608, ("B", "b"): 992, ("C", "a"): 608, ("C", "b"): 992}
+ODD = {("A", "a"): 0, ("A", "b"): 304, ("B", "a"): 1664, ("B", "b"): 1280, ("C", "a"): 1664, ("C", "b"): 1376}
 WIDTH = LIST * BLOCK + BLOCK
 OWN_WIDTH = OWN * BLOCK
 NT = (((1,), (1,)), ((), ()))

time: 115 us -> 114 us (level)
  no operation moved by 1% of the time
where the time goes in v5:
time: 114 us
  Pallas kernels  114 us (100%)
    pallas_call x1, Pallas kernels, per_device(): pl.pallas_call(kernel, out_shape=(jax.ShapeDtypeStruct((BANDS, OWN, BLOCK...  109 us
    pallas_call x1, Pallas kernels, per_device(): pl.pallas_call(divide, out_shape=jax.ShapeDtypeStruct((BANDS, OWN, BLOCK,...  4.73 us

profile of v5, /device:TPU:1, one launch (start us, length us, event | category | flops | bytes accessed | tf_op | source)
XLA Modules:
  0.0 114.0 jit_solution(7341031498094557514)
XLA Ops:
  0.0 109.3 %shard_map.37 = (f32[16,4,128,128]{3,2,1,0:T(8,128)}, bf16[2048,512]{1,0:T(8,128)(2,1)}, f32[16,128]{1,0:T(8,128)}, f32[16,4,128]{2,1,0:T(4,128)}) custom-call(bf16[16,128,128]{2,1,0:T(8,128)(2,1)} %x_ref.1, s32[4,4,1024]{2,1,0:T(4,128)} %bitcast.2, s32[4,4,1024]{2,1,0:T(4,128)} %bitcast.3), custom_call_target="tpu_custom_call" | custom-call | tf_op jit(solution)/shard_map/pallas_call | solution.py:364
  109.3 4.7 %shard_map.38 = f32[16,4,128,128]{3,2,1,0:T(8,128)} custom-call(f32[16,4,128,128]{3,2,1,0:T(8,128)} %get-tuple-element.9.sum_ref, bf16[2048,512]{1,0:T(8,128)(2,1)} %get-tuple-element.10.link_ref, f32[16,128]{1,0:T(8,128)} %get-tuple-element.11.own_ref, f32[16,4,128]{2,1,0:T(4,128)} %get-tuple-element.12.near_ref), custom_call_target="tpu_custom_call" | custom-call | tf_op jit(solution)/shard_map/pallas_call | solution.py:406
